TPU v7x, 32 devices: a whole 2x2x4 slice. The times are simulated.
32 devices in a mesh: groups: 2 (over x), rows: 16 (over z, y, core).
Axes of the slice: x: 2, y: 2, z: 4, core: 2. Of those that a mesh axis runs over, the one named last changes fastest.
Arguments:
- genotypes: bfloat16 [32768, 4096], P(('groups', 'rows')), parts along dimension 0, may hold values from -6 to 6
- sample_factors: float32 [32768, 64], P(('groups', 'rows')), parts along dimension 0, may hold values from -2.1213203 to 2.1213203
- snp_factors: float32 [20480, 64], P(('groups', 'rows')), parts along dimension 0, may hold values from -2.1213203 to 2.1213203
- coverage: int32 [32, 64], P('groups'), parts along dimension 0, may hold values from 0 to 159, as said below
Outputs:
- new_samples: float32 [32768, 64], P(('groups', 'rows')), parts along dimension 0
- new_snps: float32 [20480, 64], P(('groups', 'rows')), parts along dimension 0
There are 2 independent parts, one for each index of `groups`. A program takes and returns all parts, laid end to end along the dimension named above; each array names one. Nothing has to cross between parts.
Inputs may be any that keep to these rules, and one draw needn't show every extreme that they name: `coverage`: each row lists 64 distinct SNP blocks in ascending order, exactly 4 of them among blocks o * 10 to (o + 1) * 10 - 1 for every o; every SNP block is listed by at least one batch.
All inputs are finite; a program needn't handle non-finite values.
Results may differ from a plain program's by a relative error of at most 0.0067.
Values may be sent and summed in bfloat16 or wider, within the bound.
A program may use at most 128 MiB of HBM per device.

v0:
```python
import math
import jax
import jax.numpy as jnp
from jax import lax
from jax.sharding import PartitionSpec as P

ROUNDS = 2
weight_decay = 0.02


def on_device(genotypes, sample_factors, snp_factors, coverage):
    devices = lax.axis_size("rows")
    position = lax.axis_index("rows")
    samples_here = genotypes.shape[0]
    rank_width = sample_factors.shape[1]
    covered = coverage.shape[1]
    tile_size = genotypes.shape[1] // covered
    per_owner = covered // devices
    own_blocks = snp_factors.shape[0] // tile_size
    own_list = lax.dynamic_index_in_dim(coverage, position, 0, keepdims=False)
    local_list = (
        lax.dynamic_slice_in_dim(coverage, position * per_owner, per_owner, 1)
        - position * own_blocks
    )
    one_hot = (
        local_list[:, :, None] == jnp.arange(own_blocks, dtype=jnp.int32)[None, None, :]
    ).astype(jnp.float32)
    observers = jnp.sum(one_hot, axis=(0, 1))
    snp_step = 0.5 * math.sqrt(rank_width) / (samples_here * observers)
    sample_step = 0.5 * math.sqrt(rank_width) / (covered * tile_size)
    samples = sample_factors
    snps = snp_factors
    for iteration in range(ROUNDS):
        snp_bf16 = snps.astype(jnp.bfloat16).reshape(own_blocks, tile_size, rank_width)
        gathered = lax.all_gather(snp_bf16, "rows", axis=0, tiled=True)
        panels = gathered[own_list].reshape(covered * tile_size, rank_width)
        predicted = lax.dot_general(
            samples.astype(jnp.bfloat16),
            panels,
            (((1,), (1,)), ((), ())),
            preferred_element_type=jnp.float32,
        )
        residual = (genotypes.astype(jnp.float32) - predicted).astype(jnp.bfloat16)
        gradient = jnp.dot(residual, panels, preferred_element_type=jnp.float32)
        samples = (1.0 - weight_decay) * samples + sample_step * gradient
        sample_bf16 = samples.astype(jnp.bfloat16)
        predicted = lax.dot_general(
            sample_bf16, panels, (((1,), (1,)), ((), ())), preferred_element_type=jnp.float32
        )
        residual = (genotypes.astype(jnp.float32) - predicted).astype(jnp.bfloat16)
        snp_gradient = lax.dot_general(
            residual, sample_bf16, (((0,), (0,)), ((), ())), preferred_element_type=jnp.float32
        )
        incoming_terms = lax.all_to_all(
            snp_gradient.reshape(devices, per_owner, tile_size, rank_width).astype(jnp.bfloat16),
            "rows",
            split_axis=0,
            concat_axis=0,
            tiled=True,
        ).astype(jnp.float32)
        summed = jnp.einsum(
            "bpk,bptr->ktr", one_hot, incoming_terms, precision=lax.Precision.HIGHEST
        )
        snps = (1.0 - weight_decay) * snps + (snp_step[:, None, None] * summed).reshape(
            own_blocks * tile_size, rank_width
        )
    return (samples, snps)


def solution(mesh):
    placed = (
        P(("groups", "rows"), None),
        P(("groups", "rows"), None),
        P(("groups", "rows"), None),
        P("groups", None),
    )
    return jax.shard_map(
        on_device,
        mesh=mesh,
        in_specs=placed,
        out_specs=(P(("groups", "rows"), None), P(("groups", "rows"), None)),
        check_vma=False,
    )
```

profile of v0, /device:TPU:0, one launch (start us, length us, event | category | flops | bytes accessed | tf_op | source)
XLA Modules:
  0.0 190.6 jit_solution(12273409029608411657)
XLA Ops:
  7.2 0.0 all-gather.3.cloned.1.call-start
  7.2 1.1 copy.32
  8.3 0.7 convert_element_type.52
  9.0 0.0 all-gather.3.cloned.1.call-update
  9.0 0.0 copy-start
  9.0 0.0 copy-start.1
  9.0 12.1 %copy.31 = bf16[1024,4096]{0,1:T(8,128)(2,1)} copy(bf16[1024,4096]{1,0:T(8,128)(2,1)} %param.4) | data formatting | bytes 16777216 | tf_op args[0]
  21.1 0.0 copy-done
  21.1 35.6 %all-gather.3.cloned.1.call-done = bf16[160,64,64]{2,1,0:T(8,128)(2,1)} async-done(((bf16[10,64,64]{2,1,0:T(8,128)(2,1)}), bf16[160,64,64]{2,1,0:T(8,128)(2,1)}) %all-gather.3.cloned.1.call-update) | async-done | bytes 1310736 | tf_op jit(solution)/shard_map/all_gather | solution.py:35
  56.8 2.5 %gather_fusion = bf16[64,64,64]{2,1,0:T(8,128)(2,1)S(1)} fusion(bf16[160,64,64]{2,1,0:T(8,128)(2,1)} %all-gather.3.cloned.1.call-done, s32[1024]{0:T(1024)S(1)} %pad_clamp_fusion), kind=kCustom, calls=%fused_computation | custom fusion | bytes 1048832 | tf_op jit(solution)/shard_map/gather | solution.py:36
  59.3 0.0 copy-done.1
  59.3 7.2 %fusion.11 = f32[1024,64]{0,1:T(8,128)S(1)} fusion(bf16[4096,64]{1,0:T(8,128)(2,1)S(1)} %bitcast.58, bf16[1024,4096]{0,1:T(8,128)(2,1)} %copy.31, f32[1024,64]{0,1:T(8,128)S(1)} %copy-done.1), kind=kOutput, calls=%fused_computation.21 | convolution fusion | flops 1086586880 | bytes 9437184 | tf_op jit(solution)/shard_map/dot_general | solution.py:44
  66.5 8.1 %convolution_convert_fusion.1 = bf16[4096,64]{0,1:T(8,128)(2,1)S(1)} fusion(bf16[1024,4096]{0,1:T(8,128)(2,1)} %copy.31, bf16[4096,64]{1,0:T(8,128)(2,1)S(1)} %bitcast.59, f32[1024,64]{0,1:T(8,128)S(1)} %fusion.11), kind=kOutput, calls=%fused_computation.11 | convolution fusion | flops 1086717952 | bytes 9699328 | tf_op jit(solution)/shard_map/dot_general | solution.py:51
  74.6 1.1 convert_element_type.59
  75.7 1.9 copy.36
  77.6 1.5 reshape.84
  79.2 3.6 %all-to-all-start = ((bf16[16,2,8192]{2,1,0:T(2,128)(2,1)}), bf16[16,2,8192]{2,1,0:T(2,128)(2,1)S(1)}, u32[]{:S(2)}, u32[]{:S(2)}) async-start(bf16[16,2,8192]{2,1,0:T(2,128)(2,1)} %reshape.84), calls=%async_computation | async-start | bytes 1048576 | tf_op jit(solution)/shard_map/all_to_all | solution.py:54
  82.8 0.2 all-gather.5.cloned.1.call-start
  83.0 0.1 constant_dynamic-slice_fusion
  83.1 0.1 copy.50
  83.2 0.1 convert_reduce_fusion
  83.3 13.9 %all-to-all-done = bf16[16,2,8192]{2,1,0:T(2,128)(2,1)S(1)} async-done(((bf16[16,2,8192]{2,1,0:T(2,128)(2,1)}), bf16[16,2,8192]{2,1,0:T(2,128)(2,1)S(1)}, u32[]{:S(2)}, u32[]{:S(2)}) %all-to-all-start) | async-done | bytes 524320 | tf_op jit(solution)/shard_map/all_to_all | solution.py:54
  97.2 0.7 reshape.85
  97.9 0.7 fusion.7
  98.6 0.1 copy.38
  98.7 0.7 fusion.18
  99.4 0.0 all-gather.5.cloned.1.call-update
  99.4 42.7 %all-gather.5.cloned.1.call-done = bf16[160,64,64]{2,1,0:T(8,128)(2,1)} async-done(((bf16[10,64,64]{2,1,0:T(8,128)(2,1)}), bf16[160,64,64]{2,1,0:T(8,128)(2,1)}) %all-gather.5.cloned.1.call-update) | async-done | bytes 1310736 | tf_op jit(solution)/shard_map/all_gather | solution.py:35
  142.1 2.5 %gather_fusion.1 = bf16[64,64,64]{2,1,0:T(8,128)(2,1)S(1)} fusion(bf16[160,64,64]{2,1,0:T(8,128)(2,1)} %all-gather.5.cloned.1.call-done, s32[1024]{0:T(1024)S(1)} %pad_clamp_fusion), kind=kCustom, calls=%fused_computation.1 | custom fusion | bytes 1048832 | tf_op jit(solution)/shard_map/gather | solution.py:36
  144.6 7.1 %fusion.10 = f32[1024,64]{0,1:T(8,128)S(1)} fusion(bf16[4096,64]{1,0:T(8,128)(2,1)S(1)} %bitcast.56, bf16[1024,4096]{0,1:T(8,128)(2,1)} %copy.31, f32[1024,64]{0,1:T(8,128)S(1)} %fusion.11), kind=kOutput, calls=%fused_computation.20 | convolution fusion | flops 1086586880 | bytes 9437184 | tf_op jit(solution)/shard_map/dot_general | solution.py:44
  151.7 0.0 copy-start.2
  151.7 8.2 %convolution_convert_fusion = bf16[4096,64]{0,1:T(8,128)(2,1)S(1)} fusion(bf16[1024,4096]{0,1:T(8,128)(2,1)} %copy.31, bf16[4096,64]{1,0:T(8,128)(2,1)S(1)} %bitcast.57, f32[1024,64]{0,1:T(8,128)S(1)} %fusion.10), kind=kOutput, calls=%fused_computation.10 | convolution fusion | flops 1086717952 | bytes 9699328 | tf_op jit(solution)/shard_map/dot_general | solution.py:51
  160.0 1.1 convert_element_type.65
  161.1 1.9 copy.41
  163.0 0.7 reshape.86
  163.7 0.0 copy-done.2
  163.7 17.6 %all_to_all.10 = bf16[16,2,8192]{2,1,0:T(2,128)(2,1)S(1)} all-to-all(bf16[16,2,8192]{2,1,0:T(2,128)(2,1)S(1)} %reshape.86), channel_id=1, replica_groups=mesh['groups'=2,'rows'=16] {'rows'}, dimensions={0} | all-to-all | bytes 1048576 | tf_op jit(solution)/shard_map/all_to_all | solution.py:54
  181.4 0.7 reshape.87
  182.0 0.7 fusion.6
  182.7 0.1 copy.43
  182.8 0.1 bitcast_add_fusion
  182.9 0.8 copy.44
  (4 shorter events, 0.0 us)
Async XLA Ops:
  7.2 49.6 %all-gather.3.cloned.1.call-start = ((), (), s32[]{:S(2)}) async-start(), calls=%async_computation.2 | async-start | bytes 2785280 | tf_op jit(solution)/shard_map/all_gather | solution.py:35
  9.0 12.1 %copy-start = (s32[16,64]{1,0:T(8,128)S(1)}, s32[16,64]{1,0:T(8,128)}, u32[]{:S(2)}) copy-start(s32[16,64]{1,0:T(8,128)} %param.7) | copy-start | bytes 12292
  9.0 50.3 %copy-start.1 = (f32[1024,64]{0,1:T(8,128)S(1)}, f32[1024,64]{0,1:T(8,128)}, u32[]{:S(2)}) copy-start(f32[1024,64]{0,1:T(8,128)} %param.5) | copy-start | bytes 786436
  79.2 18.0 %all-to-all-start = ((bf16[16,2,8192]{2,1,0:T(2,128)(2,1)}), bf16[16,2,8192]{2,1,0:T(2,128)(2,1)S(1)}, u32[]{:S(2)}, u32[]{:S(2)}) async-start(bf16[16,2,8192]{2,1,0:T(2,128)(2,1)} %reshape.84), calls=%async_computation | async-start | bytes 1048576 | tf_op jit(solution)/shard_map/all_to_all | solution.py:54
  82.8 59.3 %all-gather.5.cloned.1.call-start = ((), (), s32[]{:S(2)}) async-start(), calls=%async_computation.3 | async-start | bytes 2785280 | tf_op jit(solution)/shard_map/all_gather | solution.py:35
  151.7 12.0 %copy-start.2 = (f32[1024,64]{0,1:T(8,128)}, f32[1024,64]{0,1:T(8,128)S(1)}, u32[]{:S(2)}) copy-start(f32[1024,64]{0,1:T(8,128)S(1)} %fusion.10) | copy-start | bytes 786436
Sparse Core Ops, SparseCore 0:
  10.9 45.8 all-gather.2
  99.5 42.4 all-gather.4
where the time goes:
time: 191 us
  waiting for transfers between devices  92.2 us (48%)
  matrix products  32.1 us (17%)
  local copies, waits for them, and re-layouts  29 us (15%)
  blocking collectives  17.6 us (9%)
  between operations  14.2 us (7%)
  starting transfers between devices  3.83 us (2%)
    all_gather x2, waiting for transfers between devices, on_device(): gathered = lax.all_gather(snp_bf16, 'rows', axis=0, tiled=True)  78.3 us
    unnamed x14, local copies, waits for them, and re-layouts  17.6 us
    all_to_all x1, blocking collectives, on_device(): lax.all_to_all(snp_gradient.reshape(devices, per_owner, tile_size, rank_w...  17.6 us
    dot_general x2, matrix products, on_device(): lax.dot_general(residual, sample_bf16, (((0,), (0,)), ((), ())), preferre...  16.4 us
    dot_general x2, matrix products, on_device(): gradient = jnp.dot(residual, panels, preferred_element_type=jnp.float32)  14.3 us
    all_to_all x1, waiting for transfers between devices, on_device(): lax.all_to_all(snp_gradient.reshape(devices, per_owner, tile_size, rank_w...  13.9 us
    convert_element_type x4, local copies, waits for them, and re-layouts, on_device(): snp_gradient.reshape(devices, per_owner, tile_size, rank_width)  6.07 us
    gather x2, local copies, waits for them, and re-layouts, on_device(): panels = gathered[own_list].reshape(covered * tile_size, rank_width)  4.97 us
  transfers between devices with their start and end apart: 3, of which 3 were waited for; matrix products, arithmetic and copies ran while one was open for 7% of the time, Pallas kernels for 0%

commit v1 on v0

--- a/solution.py
+++ b/solution.py
@@ -32,7 +32,25 @@
     snps = snp_factors
     for iteration in range(ROUNDS):
         snp_bf16 = snps.astype(jnp.bfloat16).reshape(own_blocks, tile_size, rank_width)
-        gathered = lax.all_gather(snp_bf16, "rows", axis=0, tiled=True)
+        ways, here, step = (lax.axis_size("rows"), lax.axis_index("rows"), snp_bf16.shape[0])
+        shape = [n * ways if d == 0 else n for d, n in enumerate(snp_bf16.shape)]
+        full = lax.dynamic_update_slice_in_dim(
+            jnp.zeros(shape, snp_bf16.dtype), snp_bf16, here * step, axis=0
+        )
+        going_up = going_down = snp_bf16
+        for far in range(1, ways // 2 + 1):
+            going_up = lax.ppermute(going_up, "rows", [(d, (d + 1) % ways) for d in range(ways)])
+            full = lax.dynamic_update_slice_in_dim(
+                full, going_up, (here - far) % ways * step, axis=0
+            )
+            if 2 * far < ways:
+                going_down = lax.ppermute(
+                    going_down, "rows", [(d, (d - 1) % ways) for d in range(ways)]
+                )
+                full = lax.dynamic_update_slice_in_dim(
+                    full, going_down, (here + far) % ways * step, axis=0
+                )
+        gathered = full
         panels = gathered[own_list].reshape(covered * tile_size, rank_width)
         predicted = lax.dot_general(
             samples.astype(jnp.bfloat16),

time: 191 us -> 217 us (1.14)
  starting transfers between devices: 3.83 us -> 68 us
  waiting for transfers between devices: 92.2 us -> 66.3 us
  between operations: 14.2 us -> 1.16 us
    all_gather x2 -> x0, waiting for transfers between devices: 78.3 us -> none  [on_device(): gathered = lax.all_gather(snp_bf16, 'rows', axis=0, tiled=True)]
    ppermute x0 -> x30, starting transfers between devices: none -> 64.5 us  [the longest x14 63.8 us: on_device(): lax.ppermute(going_down, 'rows', [(d, (d - 1) % ways) for d in range(ways)])]
    ppermute x0 -> x30, waiting for transfers between devices: none -> 52.2 us  [the longest x16 52.1 us: on_device(): lax.ppermute(going_up, 'rows', [(d, (d + 1) % ways) for d in range(ways)])]
    unnamed x14 -> x20, local copies, waits for them, and re-layouts: 17.6 us -> 18.3 us
  transfers between devices with their start and end apart: 3 -> 31, of which waited for: 3 -> 16; matrix products, arithmetic and copies ran while one was open for 7% -> 7% of each run, Pallas kernels for 0% -> 0%
where the time goes in v1:
time: 217 us
  starting transfers between devices  68 us (31%)
  waiting for transfers between devices  66.3 us (31%)
  matrix products  33.8 us (16%)
  local copies, waits for them, and re-layouts  30.1 us (14%)
  blocking collectives  17.1 us (8%)
    ppermute x14, starting transfers between devices, on_device(): lax.ppermute(going_down, 'rows', [(d, (d - 1) % ways) for d in range(ways)])  63.8 us
    ppermute x16, waiting for transfers between devices, on_device(): lax.ppermute(going_up, 'rows', [(d, (d + 1) % ways) for d in range(ways)])  52.1 us
    unnamed x20, local copies, waits for them, and re-layouts  18.3 us
    all_to_all x1, blocking collectives, on_device(): lax.all_to_all(snp_gradient.reshape(devices, per_owner, tile_size, rank_w...  17.1 us
    dot_general x2, matrix products, on_device(): lax.dot_general(residual, sample_bf16, (((0,), (0,)), ((), ())), preferre...  16.4 us
    dot_general x2, matrix products, on_device(): gradient = jnp.dot(residual, panels, preferred_element_type=jnp.float32)  16 us
    all_to_all x1, waiting for transfers between devices, on_device(): lax.all_to_all(snp_gradient.reshape(devices, per_owner, tile_size, rank_w...  14.1 us
    convert_element_type x4, local copies, waits for them, and re-layouts, on_device(): snp_gradient.reshape(devices, per_owner, tile_size, rank_width)  6.06 us
  transfers between devices with their start and end apart: 31, of which 16 were waited for; matrix products, arithmetic and copies ran while one was open for 7% of the time, Pallas kernels for 0%

profile of v1, /device:TPU:0, one launch (start us, length us, event | category | flops | bytes accessed | tf_op | source)
XLA Modules:
  0.0 216.8 jit_solution(9825041600872774595)
XLA Ops:
  0.6 1.1 copy.32
  2.2 5.1 %collective-permute-start.1 = (bf16[10,64,64]{2,1,0:T(8,128)(2,1)S(1)}, bf16[10,64,64]{2,1,0:T(8,128)(2,1)S(1)}, u32[]{:S(2)}, u32[]{:S(2)}) collective-permute-start(bf16[10,64,64]{2,1,0:T(8,128)(2,1)S(1)} %bitcast.63), channel_id=1, source_target_pairs={{0,15},{1,0},{2,1},{3,2},{4,3},{5,4},{6,5},{7,6},{8,7},{9,8},{10,9... | collective-permute-start | bytes 245768 | tf_op jit(solution)/shard_map/ppermute | solution.py:47
  7.3 12.0 %copy.31 = bf16[1024,4096]{0,1:T(8,128)(2,1)} copy(bf16[1024,4096]{1,0:T(8,128)(2,1)} %param.4) | data formatting | bytes 16777216 | tf_op args[0]
  20.2 4.4 %collective-permute-start.3 = (bf16[10,64,64]{2,1,0:T(8,128)(2,1)S(1)}, bf16[10,64,64]{2,1,0:T(8,128)(2,1)S(1)}, u32[]{:S(2)}, u32[]{:S(2)}) collective-permute-start(bf16[10,64,64]{2,1,0:T(8,128)(2,1)S(1)} %collective-permute-done.1), channel_id=1, source_target_pairs={{0,15},{1,0},{2,1},{3,2},{4,3},{5,4},{6,5},{7,6},{8,7},{9,8},{10,9... | collective-permute-start | bytes 245768 | tf_op jit(solution)/shard_map/ppermute | solution.py:47
  24.7 2.9 %collective-permute-done.2 = bf16[10,64,64]{2,1,0:T(8,128)(2,1)S(1)} collective-permute-done((bf16[10,64,64]{2,1,0:T(8,128)(2,1)S(1)}, bf16[10,64,64]{2,1,0:T(8,128)(2,1)S(1)}, u32[]{:S(2)}, u32[]{:S(2)}) %collective-permute-start.2) | collective-permute-done | bytes 81952 | tf_op jit(solution)/shard_map/ppermute | solution.py:42
  27.6 4.5 %collective-permute-start.5 = (bf16[10,64,64]{2,1,0:T(8,128)(2,1)S(1)}, bf16[10,64,64]{2,1,0:T(8,128)(2,1)S(1)}, u32[]{:S(2)}, u32[]{:S(2)}) collective-permute-start(bf16[10,64,64]{2,1,0:T(8,128)(2,1)S(1)} %collective-permute-done.3), channel_id=1, source_target_pairs={{0,15},{1,0},{2,1},{3,2},{4,3},{5,4},{6,5},{7,6},{8,7},{9,8},{10,9... | collective-permute-start | bytes 245768 | tf_op jit(solution)/shard_map/ppermute | solution.py:47
  32.2 2.9 %collective-permute-done.4 = bf16[10,64,64]{2,1,0:T(8,128)(2,1)S(1)} collective-permute-done((bf16[10,64,64]{2,1,0:T(8,128)(2,1)S(1)}, bf16[10,64,64]{2,1,0:T(8,128)(2,1)S(1)}, u32[]{:S(2)}, u32[]{:S(2)}) %collective-permute-start.4) | collective-permute-done | bytes 81952 | tf_op jit(solution)/shard_map/ppermute | solution.py:42
  35.2 4.4 %collective-permute-start.7 = (bf16[10,64,64]{2,1,0:T(8,128)(2,1)S(1)}, bf16[10,64,64]{2,1,0:T(8,128)(2,1)S(1)}, u32[]{:S(2)}, u32[]{:S(2)}) collective-permute-start(bf16[10,64,64]{2,1,0:T(8,128)(2,1)S(1)} %collective-permute-done.5), channel_id=1, source_target_pairs={{0,15},{1,0},{2,1},{3,2},{4,3},{5,4},{6,5},{7,6},{8,7},{9,8},{10,9... | collective-permute-start | bytes 245768 | tf_op jit(solution)/shard_map/ppermute | solution.py:47
  39.7 3.0 %collective-permute-done.6 = bf16[10,64,64]{2,1,0:T(8,128)(2,1)S(1)} collective-permute-done((bf16[10,64,64]{2,1,0:T(8,128)(2,1)S(1)}, bf16[10,64,64]{2,1,0:T(8,128)(2,1)S(1)}, u32[]{:S(2)}, u32[]{:S(2)}) %collective-permute-start.6) | collective-permute-done | bytes 81952 | tf_op jit(solution)/shard_map/ppermute | solution.py:42
  42.7 4.4 %collective-permute-start.9 = (bf16[10,64,64]{2,1,0:T(8,128)(2,1)S(1)}, bf16[10,64,64]{2,1,0:T(8,128)(2,1)S(1)}, u32[]{:S(2)}, u32[]{:S(2)}) collective-permute-start(bf16[10,64,64]{2,1,0:T(8,128)(2,1)S(1)} %collective-permute-done.7), channel_id=1, source_target_pairs={{0,15},{1,0},{2,1},{3,2},{4,3},{5,4},{6,5},{7,6},{8,7},{9,8},{10,9... | collective-permute-start | bytes 245768 | tf_op jit(solution)/shard_map/ppermute | solution.py:47
  47.2 3.0 %collective-permute-done.8 = bf16[10,64,64]{2,1,0:T(8,128)(2,1)S(1)} collective-permute-done((bf16[10,64,64]{2,1,0:T(8,128)(2,1)S(1)}, bf16[10,64,64]{2,1,0:T(8,128)(2,1)S(1)}, u32[]{:S(2)}, u32[]{:S(2)}) %collective-permute-start.8) | collective-permute-done | bytes 81952 | tf_op jit(solution)/shard_map/ppermute | solution.py:42
  50.3 4.4 %collective-permute-start.11 = (bf16[10,64,64]{2,1,0:T(8,128)(2,1)S(1)}, bf16[10,64,64]{2,1,0:T(8,128)(2,1)S(1)}, u32[]{:S(2)}, u32[]{:S(2)}) collective-permute-start(bf16[10,64,64]{2,1,0:T(8,128)(2,1)S(1)} %collective-permute-done.9), channel_id=1, source_target_pairs={{0,15},{1,0},{2,1},{3,2},{4,3},{5,4},{6,5},{7,6},{8,7},{9,8},{10,9... | collective-permute-start | bytes 245768 | tf_op jit(solution)/shard_map/ppermute | solution.py:47
  54.8 3.0 %collective-permute-done.10 = bf16[10,64,64]{2,1,0:T(8,128)(2,1)S(1)} collective-permute-done((bf16[10,64,64]{2,1,0:T(8,128)(2,1)S(1)}, bf16[10,64,64]{2,1,0:T(8,128)(2,1)S(1)}, u32[]{:S(2)}, u32[]{:S(2)}) %collective-permute-start.10) | collective-permute-done | bytes 81952 | tf_op jit(solution)/shard_map/ppermute | solution.py:42
  57.8 4.4 %collective-permute-start.13 = (bf16[10,64,64]{2,1,0:T(8,128)(2,1)S(1)}, bf16[10,64,64]{2,1,0:T(8,128)(2,1)S(1)}, u32[]{:S(2)}, u32[]{:S(2)}) collective-permute-start(bf16[10,64,64]{2,1,0:T(8,128)(2,1)S(1)} %collective-permute-done.11), channel_id=1, source_target_pairs={{0,15},{1,0},{2,1},{3,2},{4,3},{5,4},{6,5},{7,6},{8,7},{9,8},{10,9... | collective-permute-start | bytes 245768 | tf_op jit(solution)/shard_map/ppermute | solution.py:47
  62.3 2.9 %collective-permute-done.12 = bf16[10,64,64]{2,1,0:T(8,128)(2,1)S(1)} collective-permute-done((bf16[10,64,64]{2,1,0:T(8,128)(2,1)S(1)}, bf16[10,64,64]{2,1,0:T(8,128)(2,1)S(1)}, u32[]{:S(2)}, u32[]{:S(2)}) %collective-permute-start.12) | collective-permute-done | bytes 81952 | tf_op jit(solution)/shard_map/ppermute | solution.py:42
  65.3 7.4 %collective-permute-done.14 = bf16[10,64,64]{2,1,0:T(8,128)(2,1)S(1)} collective-permute-done((bf16[10,64,64]{2,1,0:T(8,128)(2,1)S(1)}, bf16[10,64,64]{2,1,0:T(8,128)(2,1)S(1)}, u32[]{:S(2)}, u32[]{:S(2)}) %collective-permute-start.14) | collective-permute-done | bytes 81952 | tf_op jit(solution)/shard_map/ppermute | solution.py:42
  72.7 1.7 gather_fusion
  74.4 7.9 %fusion.11 = f32[1024,64]{0,1:T(8,128)S(1)} fusion(bf16[4096,64]{1,0:T(8,128)(2,1)} %bitcast.60, bf16[1024,4096]{0,1:T(8,128)(2,1)} %copy.31, f32[1024,64]{0,1:T(8,128)S(1)} %copy-done.3), kind=kOutput, calls=%fused_computation.21 | convolution fusion | flops 1086586880 | bytes 9437184 | tf_op jit(solution)/shard_map/dot_general | solution.py:62
  83.0 8.1 %convolution_convert_fusion.1 = bf16[4096,64]{0,1:T(8,128)(2,1)S(1)} fusion(bf16[1024,4096]{0,1:T(8,128)(2,1)} %copy.31, bf16[4096,64]{1,0:T(8,128)(2,1)S(1)} %bitcast.61, f32[1024,64]{0,1:T(8,128)S(1)} %fusion.11), kind=kOutput, calls=%fused_computation.11 | convolution fusion | flops 1086717952 | bytes 9699328 | tf_op jit(solution)/shard_map/dot_general | solution.py:69
  91.2 1.1 convert_element_type.59
  92.3 1.9 copy.36
  94.2 1.6 reshape.84
  95.8 3.6 %all-to-all-start = ((bf16[16,2,8192]{2,1,0:T(2,128)(2,1)}), bf16[16,2,8192]{2,1,0:T(2,128)(2,1)S(1)}, u32[]{:S(2)}, u32[]{:S(2)}) async-start(bf16[16,2,8192]{2,1,0:T(2,128)(2,1)} %reshape.84), calls=%async_computation | async-start | bytes 1048576 | tf_op jit(solution)/shard_map/all_to_all | solution.py:72
  99.7 14.1 %all-to-all-done = bf16[16,2,8192]{2,1,0:T(2,128)(2,1)S(1)} async-done(((bf16[16,2,8192]{2,1,0:T(2,128)(2,1)}), bf16[16,2,8192]{2,1,0:T(2,128)(2,1)S(1)}, u32[]{:S(2)}, u32[]{:S(2)}) %all-to-all-start) | async-done | bytes 524320 | tf_op jit(solution)/shard_map/all_to_all | solution.py:72
  114.5 0.7 fusion.7
  115.4 4.4 %collective-permute-start.16 = (bf16[10,64,64]{2,1,0:T(8,128)(2,1)S(1)}, bf16[10,64,64]{2,1,0:T(8,128)(2,1)S(1)}, u32[]{:S(2)}, u32[]{:S(2)}) collective-permute-start(bf16[10,64,64]{2,1,0:T(8,128)(2,1)S(1)} %bitcast.66), channel_id=1, source_target_pairs={{0,15},{1,0},{2,1},{3,2},{4,3},{5,4},{6,5},{7,6},{8,7},{9,8},{10,9... | collective-permute-start | bytes 245768 | tf_op jit(solution)/shard_map/ppermute | solution.py:47
  120.5 2.3 %collective-permute-done.15 = bf16[10,64,64]{2,1,0:T(8,128)(2,1)S(1)} collective-permute-done((bf16[10,64,64]{2,1,0:T(8,128)(2,1)S(1)}, bf16[10,64,64]{2,1,0:T(8,128)(2,1)S(1)}, u32[]{:S(2)}, u32[]{:S(2)}) %collective-permute-start.15) | collective-permute-done | bytes 81952 | tf_op jit(solution)/shard_map/ppermute | solution.py:42
  122.9 4.5 %collective-permute-start.18 = (bf16[10,64,64]{2,1,0:T(8,128)(2,1)S(1)}, bf16[10,64,64]{2,1,0:T(8,128)(2,1)S(1)}, u32[]{:S(2)}, u32[]{:S(2)}) collective-permute-start(bf16[10,64,64]{2,1,0:T(8,128)(2,1)S(1)} %collective-permute-done.16), channel_id=1, source_target_pairs={{0,15},{1,0},{2,1},{3,2},{4,3},{5,4},{6,5},{7,6},{8,7},{9,8},{10,9... | collective-permute-start | bytes 245768 | tf_op jit(solution)/shard_map/ppermute | solution.py:47
  127.4 3.0 %collective-permute-done.17 = bf16[10,64,64]{2,1,0:T(8,128)(2,1)S(1)} collective-permute-done((bf16[10,64,64]{2,1,0:T(8,128)(2,1)S(1)}, bf16[10,64,64]{2,1,0:T(8,128)(2,1)S(1)}, u32[]{:S(2)}, u32[]{:S(2)}) %collective-permute-start.17) | collective-permute-done | bytes 81952 | tf_op jit(solution)/shard_map/ppermute | solution.py:42
  130.4 4.7 %collective-permute-start.20 = (bf16[10,64,64]{2,1,0:T(8,128)(2,1)S(1)}, bf16[10,64,64]{2,1,0:T(8,128)(2,1)S(1)}, u32[]{:S(2)}, u32[]{:S(2)}) collective-permute-start(bf16[10,64,64]{2,1,0:T(8,128)(2,1)S(1)} %collective-permute-done.18), channel_id=1, source_target_pairs={{0,15},{1,0},{2,1},{3,2},{4,3},{5,4},{6,5},{7,6},{8,7},{9,8},{10,9... | collective-permute-start | bytes 245768 | tf_op jit(solution)/shard_map/ppermute | solution.py:47
  135.1 2.8 %collective-permute-done.19 = bf16[10,64,64]{2,1,0:T(8,128)(2,1)S(1)} collective-permute-done((bf16[10,64,64]{2,1,0:T(8,128)(2,1)S(1)}, bf16[10,64,64]{2,1,0:T(8,128)(2,1)S(1)}, u32[]{:S(2)}, u32[]{:S(2)}) %collective-permute-start.19) | collective-permute-done | bytes 81952 | tf_op jit(solution)/shard_map/ppermute | solution.py:42
  137.9 4.6 %collective-permute-start.22 = (bf16[10,64,64]{2,1,0:T(8,128)(2,1)S(1)}, bf16[10,64,64]{2,1,0:T(8,128)(2,1)S(1)}, u32[]{:S(2)}, u32[]{:S(2)}) collective-permute-start(bf16[10,64,64]{2,1,0:T(8,128)(2,1)S(1)} %collective-permute-done.20), channel_id=1, source_target_pairs={{0,15},{1,0},{2,1},{3,2},{4,3},{5,4},{6,5},{7,6},{8,7},{9,8},{10,9... | collective-permute-start | bytes 245768 | tf_op jit(solution)/shard_map/ppermute | solution.py:47
  142.6 2.9 %collective-permute-done.21 = bf16[10,64,64]{2,1,0:T(8,128)(2,1)S(1)} collective-permute-done((bf16[10,64,64]{2,1,0:T(8,128)(2,1)S(1)}, bf16[10,64,64]{2,1,0:T(8,128)(2,1)S(1)}, u32[]{:S(2)}, u32[]{:S(2)}) %collective-permute-start.21) | collective-permute-done | bytes 81952 | tf_op jit(solution)/shard_map/ppermute | solution.py:42
  145.5 4.6 %collective-permute-start.24 = (bf16[10,64,64]{2,1,0:T(8,128)(2,1)S(1)}, bf16[10,64,64]{2,1,0:T(8,128)(2,1)S(1)}, u32[]{:S(2)}, u32[]{:S(2)}) collective-permute-start(bf16[10,64,64]{2,1,0:T(8,128)(2,1)S(1)} %collective-permute-done.22), channel_id=1, source_target_pairs={{0,15},{1,0},{2,1},{3,2},{4,3},{5,4},{6,5},{7,6},{8,7},{9,8},{10,9... | collective-permute-start | bytes 245768 | tf_op jit(solution)/shard_map/ppermute | solution.py:47
  150.1 2.9 %collective-permute-done.23 = bf16[10,64,64]{2,1,0:T(8,128)(2,1)S(1)} collective-permute-done((bf16[10,64,64]{2,1,0:T(8,128)(2,1)S(1)}, bf16[10,64,64]{2,1,0:T(8,128)(2,1)S(1)}, u32[]{:S(2)}, u32[]{:S(2)}) %collective-permute-start.23) | collective-permute-done | bytes 81952 | tf_op jit(solution)/shard_map/ppermute | solution.py:42
  153.0 4.6 %collective-permute-start.26 = (bf16[10,64,64]{2,1,0:T(8,128)(2,1)S(1)}, bf16[10,64,64]{2,1,0:T(8,128)(2,1)S(1)}, u32[]{:S(2)}, u32[]{:S(2)}) collective-permute-start(bf16[10,64,64]{2,1,0:T(8,128)(2,1)S(1)} %collective-permute-done.24), channel_id=1, source_target_pairs={{0,15},{1,0},{2,1},{3,2},{4,3},{5,4},{6,5},{7,6},{8,7},{9,8},{10,9... | collective-permute-start | bytes 245768 | tf_op jit(solution)/shard_map/ppermute | solution.py:47
  157.7 2.9 %collective-permute-done.25 = bf16[10,64,64]{2,1,0:T(8,128)(2,1)S(1)} collective-permute-done((bf16[10,64,64]{2,1,0:T(8,128)(2,1)S(1)}, bf16[10,64,64]{2,1,0:T(8,128)(2,1)S(1)}, u32[]{:S(2)}, u32[]{:S(2)}) %collective-permute-start.25) | collective-permute-done | bytes 81952 | tf_op jit(solution)/shard_map/ppermute | solution.py:42
  160.6 4.6 %collective-permute-start.28 = (bf16[10,64,64]{2,1,0:T(8,128)(2,1)S(1)}, bf16[10,64,64]{2,1,0:T(8,128)(2,1)S(1)}, u32[]{:S(2)}, u32[]{:S(2)}) collective-permute-start(bf16[10,64,64]{2,1,0:T(8,128)(2,1)S(1)} %collective-permute-done.26), channel_id=1, source_target_pairs={{0,15},{1,0},{2,1},{3,2},{4,3},{5,4},{6,5},{7,6},{8,7},{9,8},{10,9... | collective-permute-start | bytes 245768 | tf_op jit(solution)/shard_map/ppermute | solution.py:47
  165.2 2.8 %collective-permute-done.27 = bf16[10,64,64]{2,1,0:T(8,128)(2,1)S(1)} collective-permute-done((bf16[10,64,64]{2,1,0:T(8,128)(2,1)S(1)}, bf16[10,64,64]{2,1,0:T(8,128)(2,1)S(1)}, u32[]{:S(2)}, u32[]{:S(2)}) %collective-permute-start.27) | collective-permute-done | bytes 81952 | tf_op jit(solution)/shard_map/ppermute | solution.py:42
  168.1 7.4 %collective-permute-done.29 = bf16[10,64,64]{2,1,0:T(8,128)(2,1)S(1)} collective-permute-done((bf16[10,64,64]{2,1,0:T(8,128)(2,1)S(1)}, bf16[10,64,64]{2,1,0:T(8,128)(2,1)S(1)}, u32[]{:S(2)}, u32[]{:S(2)}) %collective-permute-start.29) | collective-permute-done | bytes 81952 | tf_op jit(solution)/shard_map/ppermute | solution.py:42
  175.5 1.7 gather_fusion.1
  177.2 8.2 %fusion.10 = f32[1024,64]{0,1:T(8,128)S(1)} fusion(bf16[4096,64]{1,0:T(8,128)(2,1)} %bitcast.58, bf16[1024,4096]{0,1:T(8,128)(2,1)} %copy.31, f32[1024,64]{0,1:T(8,128)} %copy-done.5), kind=kOutput, calls=%fused_computation.20 | convolution fusion | flops 1086586880 | bytes 9437184 | tf_op jit(solution)/shard_map/dot_general | solution.py:62
  185.4 8.2 %convolution_convert_fusion = bf16[4096,64]{0,1:T(8,128)(2,1)S(1)} fusion(bf16[1024,4096]{0,1:T(8,128)(2,1)} %copy.31, bf16[4096,64]{1,0:T(8,128)(2,1)S(1)} %bitcast.59, f32[1024,64]{0,1:T(8,128)S(1)} %fusion.10), kind=kOutput, calls=%fused_computation.10 | convolution fusion | flops 1086717952 | bytes 9699328 | tf_op jit(solution)/shard_map/dot_general | solution.py:69
  193.6 1.1 convert_element_type.65
  194.7 1.9 copy.41
  196.6 0.7 reshape.86
  197.4 17.1 %all_to_all.10 = bf16[16,2,8192]{2,1,0:T(2,128)(2,1)S(1)} all-to-all(bf16[16,2,8192]{2,1,0:T(2,128)(2,1)S(1)} %reshape.86), channel_id=1, replica_groups=mesh['groups'=2,'rows'=16] {'rows'}, dimensions={0} | all-to-all | bytes 1048576 | tf_op jit(solution)/shard_map/all_to_all | solution.py:72
  216.0 0.8 copy.44
  (92 shorter events, 6.2 us)
Async XLA Ops:
  1.7 18.4 %collective-permute-start = (bf16[10,64,64]{2,1,0:T(8,128)(2,1)S(1)}, bf16[10,64,64]{2,1,0:T(8,128)(2,1)S(1)}, u32[]{:S(2)}, u32[]{:S(2)}) collective-permute-start(bf16[10,64,64]{2,1,0:T(8,128)(2,1)S(1)} %bitcast.62), channel_id=1, source_target_pairs={{0,1},{1,2},{2,3},{3,4},{4,5},{5,6},{6,7},{7,8},{8,9},{9,10},{10,1... | collective-permute-start | bytes 245768 | tf_op jit(solution)/shard_map/ppermute | solution.py:42
  2.2 17.9 %collective-permute-start.1 = (bf16[10,64,64]{2,1,0:T(8,128)(2,1)S(1)}, bf16[10,64,64]{2,1,0:T(8,128)(2,1)S(1)}, u32[]{:S(2)}, u32[]{:S(2)}) collective-permute-start(bf16[10,64,64]{2,1,0:T(8,128)(2,1)S(1)} %bitcast.63), channel_id=1, source_target_pairs={{0,15},{1,0},{2,1},{3,2},{4,3},{5,4},{6,5},{7,6},{8,7},{9,8},{10,9... | collective-permute-start | bytes 245768 | tf_op jit(solution)/shard_map/ppermute | solution.py:47
  19.3 0.8 copy-start.2
  20.1 7.5 %collective-permute-start.2 = (bf16[10,64,64]{2,1,0:T(8,128)(2,1)S(1)}, bf16[10,64,64]{2,1,0:T(8,128)(2,1)S(1)}, u32[]{:S(2)}, u32[]{:S(2)}) collective-permute-start(bf16[10,64,64]{2,1,0:T(8,128)(2,1)S(1)} %collective-permute-done), channel_id=1, source_target_pairs={{0,1},{1,2},{2,3},{3,4},{4,5},{5,6},{6,7},{7,8},{8,9},{9,10},{10,1... | collective-permute-start | bytes 245768 | tf_op jit(solution)/shard_map/ppermute | solution.py:42
  20.2 7.4 %collective-permute-start.3 = (bf16[10,64,64]{2,1,0:T(8,128)(2,1)S(1)}, bf16[10,64,64]{2,1,0:T(8,128)(2,1)S(1)}, u32[]{:S(2)}, u32[]{:S(2)}) collective-permute-start(bf16[10,64,64]{2,1,0:T(8,128)(2,1)S(1)} %collective-permute-done.1), channel_id=1, source_target_pairs={{0,15},{1,0},{2,1},{3,2},{4,3},{5,4},{6,5},{7,6},{8,7},{9,8},{10,9... | collective-permute-start | bytes 245768 | tf_op jit(solution)/shard_map/ppermute | solution.py:47
  27.6 7.5 %collective-permute-start.4 = (bf16[10,64,64]{2,1,0:T(8,128)(2,1)S(1)}, bf16[10,64,64]{2,1,0:T(8,128)(2,1)S(1)}, u32[]{:S(2)}, u32[]{:S(2)}) collective-permute-start(bf16[10,64,64]{2,1,0:T(8,128)(2,1)S(1)} %collective-permute-done.2), channel_id=1, source_target_pairs={{0,1},{1,2},{2,3},{3,4},{4,5},{5,6},{6,7},{7,8},{8,9},{9,10},{10,1... | collective-permute-start | bytes 245768 | tf_op jit(solution)/shard_map/ppermute | solution.py:42
  27.6 7.5 %collective-permute-start.5 = (bf16[10,64,64]{2,1,0:T(8,128)(2,1)S(1)}, bf16[10,64,64]{2,1,0:T(8,128)(2,1)S(1)}, u32[]{:S(2)}, u32[]{:S(2)}) collective-permute-start(bf16[10,64,64]{2,1,0:T(8,128)(2,1)S(1)} %collective-permute-done.3), channel_id=1, source_target_pairs={{0,15},{1,0},{2,1},{3,2},{4,3},{5,4},{6,5},{7,6},{8,7},{9,8},{10,9... | collective-permute-start | bytes 245768 | tf_op jit(solution)/shard_map/ppermute | solution.py:47
  35.2 7.5 %collective-permute-start.6 = (bf16[10,64,64]{2,1,0:T(8,128)(2,1)S(1)}, bf16[10,64,64]{2,1,0:T(8,128)(2,1)S(1)}, u32[]{:S(2)}, u32[]{:S(2)}) collective-permute-start(bf16[10,64,64]{2,1,0:T(8,128)(2,1)S(1)} %collective-permute-done.4), channel_id=1, source_target_pairs={{0,1},{1,2},{2,3},{3,4},{4,5},{5,6},{6,7},{7,8},{8,9},{9,10},{10,1... | collective-permute-start | bytes 245768 | tf_op jit(solution)/shard_map/ppermute | solution.py:42
  35.2 7.5 %collective-permute-start.7 = (bf16[10,64,64]{2,1,0:T(8,128)(2,1)S(1)}, bf16[10,64,64]{2,1,0:T(8,128)(2,1)S(1)}, u32[]{:S(2)}, u32[]{:S(2)}) collective-permute-start(bf16[10,64,64]{2,1,0:T(8,128)(2,1)S(1)} %collective-permute-done.5), channel_id=1, source_target_pairs={{0,15},{1,0},{2,1},{3,2},{4,3},{5,4},{6,5},{7,6},{8,7},{9,8},{10,9... | collective-permute-start | bytes 245768 | tf_op jit(solution)/shard_map/ppermute | solution.py:47
  39.6 34.8 %copy-start.3 = (f32[1024,64]{0,1:T(8,128)S(1)}, f32[1024,64]{0,1:T(8,128)}, u32[]{:S(2)}) copy-start(f32[1024,64]{0,1:T(8,128)} %param.5) | copy-start | bytes 786436
  42.7 7.5 %collective-permute-start.8 = (bf16[10,64,64]{2,1,0:T(8,128)(2,1)S(1)}, bf16[10,64,64]{2,1,0:T(8,128)(2,1)S(1)}, u32[]{:S(2)}, u32[]{:S(2)}) collective-permute-start(bf16[10,64,64]{2,1,0:T(8,128)(2,1)S(1)} %collective-permute-done.6), channel_id=1, source_target_pairs={{0,1},{1,2},{2,3},{3,4},{4,5},{5,6},{6,7},{7,8},{8,9},{9,10},{10,1... | collective-permute-start | bytes 245768 | tf_op jit(solution)/shard_map/ppermute | solution.py:42
  42.7 7.5 %collective-permute-start.9 = (bf16[10,64,64]{2,1,0:T(8,128)(2,1)S(1)}, bf16[10,64,64]{2,1,0:T(8,128)(2,1)S(1)}, u32[]{:S(2)}, u32[]{:S(2)}) collective-permute-start(bf16[10,64,64]{2,1,0:T(8,128)(2,1)S(1)} %collective-permute-done.7), channel_id=1, source_target_pairs={{0,15},{1,0},{2,1},{3,2},{4,3},{5,4},{6,5},{7,6},{8,7},{9,8},{10,9... | collective-permute-start | bytes 245768 | tf_op jit(solution)/shard_map/ppermute | solution.py:47
  50.3 7.5 %collective-permute-start.10 = (bf16[10,64,64]{2,1,0:T(8,128)(2,1)S(1)}, bf16[10,64,64]{2,1,0:T(8,128)(2,1)S(1)}, u32[]{:S(2)}, u32[]{:S(2)}) collective-permute-start(bf16[10,64,64]{2,1,0:T(8,128)(2,1)S(1)} %collective-permute-done.8), channel_id=1, source_target_pairs={{0,1},{1,2},{2,3},{3,4},{4,5},{5,6},{6,7},{7,8},{8,9},{9,10},{10,1... | collective-permute-start | bytes 245768 | tf_op jit(solution)/shard_map/ppermute | solution.py:42
  50.3 7.5 %collective-permute-start.11 = (bf16[10,64,64]{2,1,0:T(8,128)(2,1)S(1)}, bf16[10,64,64]{2,1,0:T(8,128)(2,1)S(1)}, u32[]{:S(2)}, u32[]{:S(2)}) collective-permute-start(bf16[10,64,64]{2,1,0:T(8,128)(2,1)S(1)} %collective-permute-done.9), channel_id=1, source_target_pairs={{0,15},{1,0},{2,1},{3,2},{4,3},{5,4},{6,5},{7,6},{8,7},{9,8},{10,9... | collective-permute-start | bytes 245768 | tf_op jit(solution)/shard_map/ppermute | solution.py:47
  57.8 7.4 %collective-permute-start.12 = (bf16[10,64,64]{2,1,0:T(8,128)(2,1)S(1)}, bf16[10,64,64]{2,1,0:T(8,128)(2,1)S(1)}, u32[]{:S(2)}, u32[]{:S(2)}) collective-permute-start(bf16[10,64,64]{2,1,0:T(8,128)(2,1)S(1)} %collective-permute-done.10), channel_id=1, source_target_pairs={{0,1},{1,2},{2,3},{3,4},{4,5},{5,6},{6,7},{7,8},{8,9},{9,10},{10,1... | collective-permute-start | bytes 245768 | tf_op jit(solution)/shard_map/ppermute | solution.py:42
  57.8 7.5 %collective-permute-start.13 = (bf16[10,64,64]{2,1,0:T(8,128)(2,1)S(1)}, bf16[10,64,64]{2,1,0:T(8,128)(2,1)S(1)}, u32[]{:S(2)}, u32[]{:S(2)}) collective-permute-start(bf16[10,64,64]{2,1,0:T(8,128)(2,1)S(1)} %collective-permute-done.11), channel_id=1, source_target_pairs={{0,15},{1,0},{2,1},{3,2},{4,3},{5,4},{6,5},{7,6},{8,7},{9,8},{10,9... | collective-permute-start | bytes 245768 | tf_op jit(solution)/shard_map/ppermute | solution.py:47
  65.3 7.4 %collective-permute-start.14 = (bf16[10,64,64]{2,1,0:T(8,128)(2,1)S(1)}, bf16[10,64,64]{2,1,0:T(8,128)(2,1)S(1)}, u32[]{:S(2)}, u32[]{:S(2)}) collective-permute-start(bf16[10,64,64]{2,1,0:T(8,128)(2,1)S(1)} %collective-permute-done.12), channel_id=1, source_target_pairs={{0,1},{1,2},{2,3},{3,4},{4,5},{5,6},{6,7},{7,8},{8,9},{9,10},{10,1... | collective-permute-start | bytes 245768 | tf_op jit(solution)/shard_map/ppermute | solution.py:42
  74.4 8.6 %copy-start.1 = (bf16[64,64,64]{2,1,0:T(8,128)(2,1)S(1)}, bf16[64,64,64]{2,1,0:T(8,128)(2,1)}, u32[]{:S(2)}) copy-start(bf16[64,64,64]{2,1,0:T(8,128)(2,1)} %gather_fusion) | copy-start | bytes 1572868
  82.3 0.7 copy-start.5
  95.8 18.0 %all-to-all-start = ((bf16[16,2,8192]{2,1,0:T(2,128)(2,1)}), bf16[16,2,8192]{2,1,0:T(2,128)(2,1)S(1)}, u32[]{:S(2)}, u32[]{:S(2)}) async-start(bf16[16,2,8192]{2,1,0:T(2,128)(2,1)} %reshape.84), calls=%async_computation | async-start | bytes 1048576 | tf_op jit(solution)/shard_map/all_to_all | solution.py:72
  115.3 7.5 %collective-permute-start.15 = (bf16[10,64,64]{2,1,0:T(8,128)(2,1)S(1)}, bf16[10,64,64]{2,1,0:T(8,128)(2,1)S(1)}, u32[]{:S(2)}, u32[]{:S(2)}) collective-permute-start(bf16[10,64,64]{2,1,0:T(8,128)(2,1)S(1)} %bitcast.65), channel_id=1, source_target_pairs={{0,1},{1,2},{2,3},{3,4},{4,5},{5,6},{6,7},{7,8},{8,9},{9,10},{10,1... | collective-permute-start | bytes 245768 | tf_op jit(solution)/shard_map/ppermute | solution.py:42
  115.4 7.5 %collective-permute-start.16 = (bf16[10,64,64]{2,1,0:T(8,128)(2,1)S(1)}, bf16[10,64,64]{2,1,0:T(8,128)(2,1)S(1)}, u32[]{:S(2)}, u32[]{:S(2)}) collective-permute-start(bf16[10,64,64]{2,1,0:T(8,128)(2,1)S(1)} %bitcast.66), channel_id=1, source_target_pairs={{0,15},{1,0},{2,1},{3,2},{4,3},{5,4},{6,5},{7,6},{8,7},{9,8},{10,9... | collective-permute-start | bytes 245768 | tf_op jit(solution)/shard_map/ppermute | solution.py:47
  122.8 7.5 %collective-permute-start.17 = (bf16[10,64,64]{2,1,0:T(8,128)(2,1)S(1)}, bf16[10,64,64]{2,1,0:T(8,128)(2,1)S(1)}, u32[]{:S(2)}, u32[]{:S(2)}) collective-permute-start(bf16[10,64,64]{2,1,0:T(8,128)(2,1)S(1)} %collective-permute-done.15), channel_id=1, source_target_pairs={{0,1},{1,2},{2,3},{3,4},{4,5},{5,6},{6,7},{7,8},{8,9},{9,10},{10,1... | collective-permute-start | bytes 245768 | tf_op jit(solution)/shard_map/ppermute | solution.py:42
  122.9 7.5 %collective-permute-start.18 = (bf16[10,64,64]{2,1,0:T(8,128)(2,1)S(1)}, bf16[10,64,64]{2,1,0:T(8,128)(2,1)S(1)}, u32[]{:S(2)}, u32[]{:S(2)}) collective-permute-start(bf16[10,64,64]{2,1,0:T(8,128)(2,1)S(1)} %collective-permute-done.16), channel_id=1, source_target_pairs={{0,15},{1,0},{2,1},{3,2},{4,3},{5,4},{6,5},{7,6},{8,7},{9,8},{10,9... | collective-permute-start | bytes 245768 | tf_op jit(solution)/shard_map/ppermute | solution.py:47
  130.4 7.5 %collective-permute-start.19 = (bf16[10,64,64]{2,1,0:T(8,128)(2,1)S(1)}, bf16[10,64,64]{2,1,0:T(8,128)(2,1)S(1)}, u32[]{:S(2)}, u32[]{:S(2)}) collective-permute-start(bf16[10,64,64]{2,1,0:T(8,128)(2,1)S(1)} %collective-permute-done.17), channel_id=1, source_target_pairs={{0,1},{1,2},{2,3},{3,4},{4,5},{5,6},{6,7},{7,8},{8,9},{9,10},{10,1... | collective-permute-start | bytes 245768 | tf_op jit(solution)/shard_map/ppermute | solution.py:42
  130.4 7.5 %collective-permute-start.20 = (bf16[10,64,64]{2,1,0:T(8,128)(2,1)S(1)}, bf16[10,64,64]{2,1,0:T(8,128)(2,1)S(1)}, u32[]{:S(2)}, u32[]{:S(2)}) collective-permute-start(bf16[10,64,64]{2,1,0:T(8,128)(2,1)S(1)} %collective-permute-done.18), channel_id=1, source_target_pairs={{0,15},{1,0},{2,1},{3,2},{4,3},{5,4},{6,5},{7,6},{8,7},{9,8},{10,9... | collective-permute-start | bytes 245768 | tf_op jit(solution)/shard_map/ppermute | solution.py:47
  137.9 7.5 %collective-permute-start.21 = (bf16[10,64,64]{2,1,0:T(8,128)(2,1)S(1)}, bf16[10,64,64]{2,1,0:T(8,128)(2,1)S(1)}, u32[]{:S(2)}, u32[]{:S(2)}) collective-permute-start(bf16[10,64,64]{2,1,0:T(8,128)(2,1)S(1)} %collective-permute-done.19), channel_id=1, source_target_pairs={{0,1},{1,2},{2,3},{3,4},{4,5},{5,6},{6,7},{7,8},{8,9},{9,10},{10,1... | collective-permute-start | bytes 245768 | tf_op jit(solution)/shard_map/ppermute | solution.py:42
  137.9 7.5 %collective-permute-start.22 = (bf16[10,64,64]{2,1,0:T(8,128)(2,1)S(1)}, bf16[10,64,64]{2,1,0:T(8,128)(2,1)S(1)}, u32[]{:S(2)}, u32[]{:S(2)}) collective-permute-start(bf16[10,64,64]{2,1,0:T(8,128)(2,1)S(1)} %collective-permute-done.20), channel_id=1, source_target_pairs={{0,15},{1,0},{2,1},{3,2},{4,3},{5,4},{6,5},{7,6},{8,7},{9,8},{10,9... | collective-permute-start | bytes 245768 | tf_op jit(solution)/shard_map/ppermute | solution.py:47
  145.5 7.5 %collective-permute-start.23 = (bf16[10,64,64]{2,1,0:T(8,128)(2,1)S(1)}, bf16[10,64,64]{2,1,0:T(8,128)(2,1)S(1)}, u32[]{:S(2)}, u32[]{:S(2)}) collective-permute-start(bf16[10,64,64]{2,1,0:T(8,128)(2,1)S(1)} %collective-permute-done.21), channel_id=1, source_target_pairs={{0,1},{1,2},{2,3},{3,4},{4,5},{5,6},{6,7},{7,8},{8,9},{9,10},{10,1... | collective-permute-start | bytes 245768 | tf_op jit(solution)/shard_map/ppermute | solution.py:42
  145.5 7.5 %collective-permute-start.24 = (bf16[10,64,64]{2,1,0:T(8,128)(2,1)S(1)}, bf16[10,64,64]{2,1,0:T(8,128)(2,1)S(1)}, u32[]{:S(2)}, u32[]{:S(2)}) collective-permute-start(bf16[10,64,64]{2,1,0:T(8,128)(2,1)S(1)} %collective-permute-done.22), channel_id=1, source_target_pairs={{0,15},{1,0},{2,1},{3,2},{4,3},{5,4},{6,5},{7,6},{8,7},{9,8},{10,9... | collective-permute-start | bytes 245768 | tf_op jit(solution)/shard_map/ppermute | solution.py:47
  153.0 7.5 %collective-permute-start.25 = (bf16[10,64,64]{2,1,0:T(8,128)(2,1)S(1)}, bf16[10,64,64]{2,1,0:T(8,128)(2,1)S(1)}, u32[]{:S(2)}, u32[]{:S(2)}) collective-permute-start(bf16[10,64,64]{2,1,0:T(8,128)(2,1)S(1)} %collective-permute-done.23), channel_id=1, source_target_pairs={{0,1},{1,2},{2,3},{3,4},{4,5},{5,6},{6,7},{7,8},{8,9},{9,10},{10,1... | collective-permute-start | bytes 245768 | tf_op jit(solution)/shard_map/ppermute | solution.py:42
  153.0 7.5 %collective-permute-start.26 = (bf16[10,64,64]{2,1,0:T(8,128)(2,1)S(1)}, bf16[10,64,64]{2,1,0:T(8,128)(2,1)S(1)}, u32[]{:S(2)}, u32[]{:S(2)}) collective-permute-start(bf16[10,64,64]{2,1,0:T(8,128)(2,1)S(1)} %collective-permute-done.24), channel_id=1, source_target_pairs={{0,15},{1,0},{2,1},{3,2},{4,3},{5,4},{6,5},{7,6},{8,7},{9,8},{10,9... | collective-permute-start | bytes 245768 | tf_op jit(solution)/shard_map/ppermute | solution.py:47
  160.6 7.4 %collective-permute-start.27 = (bf16[10,64,64]{2,1,0:T(8,128)(2,1)S(1)}, bf16[10,64,64]{2,1,0:T(8,128)(2,1)S(1)}, u32[]{:S(2)}, u32[]{:S(2)}) collective-permute-start(bf16[10,64,64]{2,1,0:T(8,128)(2,1)S(1)} %collective-permute-done.25), channel_id=1, source_target_pairs={{0,1},{1,2},{2,3},{3,4},{4,5},{5,6},{6,7},{7,8},{8,9},{9,10},{10,1... | collective-permute-start | bytes 245768 | tf_op jit(solution)/shard_map/ppermute | solution.py:42
  160.6 7.4 %collective-permute-start.28 = (bf16[10,64,64]{2,1,0:T(8,128)(2,1)S(1)}, bf16[10,64,64]{2,1,0:T(8,128)(2,1)S(1)}, u32[]{:S(2)}, u32[]{:S(2)}) collective-permute-start(bf16[10,64,64]{2,1,0:T(8,128)(2,1)S(1)} %collective-permute-done.26), channel_id=1, source_target_pairs={{0,15},{1,0},{2,1},{3,2},{4,3},{5,4},{6,5},{7,6},{8,7},{9,8},{10,9... | collective-permute-start | bytes 245768 | tf_op jit(solution)/shard_map/ppermute | solution.py:47
  168.0 7.4 %collective-permute-start.29 = (bf16[10,64,64]{2,1,0:T(8,128)(2,1)S(1)}, bf16[10,64,64]{2,1,0:T(8,128)(2,1)S(1)}, u32[]{:S(2)}, u32[]{:S(2)}) collective-permute-start(bf16[10,64,64]{2,1,0:T(8,128)(2,1)S(1)} %collective-permute-done.27), channel_id=1, source_target_pairs={{0,1},{1,2},{2,3},{3,4},{4,5},{5,6},{6,7},{7,8},{8,9},{9,10},{10,1... | collective-permute-start | bytes 245768 | tf_op jit(solution)/shard_map/ppermute | solution.py:42
  177.2 8.2 %copy-start = (bf16[64,64,64]{2,1,0:T(8,128)(2,1)S(1)}, bf16[64,64,64]{2,1,0:T(8,128)(2,1)}, u32[]{:S(2)}) copy-start(bf16[64,64,64]{2,1,0:T(8,128)(2,1)} %gather_fusion.1) | copy-start | bytes 1572868
  185.3 8.3 %copy-start.4 = (f32[1024,64]{0,1:T(8,128)}, f32[1024,64]{0,1:T(8,128)S(1)}, u32[]{:S(2)}) copy-start(f32[1024,64]{0,1:T(8,128)S(1)} %fusion.10) | copy-start | bytes 786436
